TPU v7x, 32 devices: a whole 2x2x4 slice. The times are simulated.
32 devices in a mesh: dom: 32 (over z, y, x, core).
Axes of the slice: x: 2, y: 2, z: 4, core: 2. Of those that a mesh axis runs over, the one named last changes fastest.
Arguments:
- node_feat: float32 [131072, 128], P('dom'), may hold values from -6 to 6
- out_grad: float32 [131072, 128], P('dom'), may hold values from -6 to 6
- lattice_of: int32 [256, 512], P('dom'), may hold values from 0 to 511, each once within a row
- element_place: int32 [32, 8], P('dom'), may hold values from 0 to 7, each once within a row
- edge_in: float32 [256, 128], replicated, may hold values from -0.375 to 0.375
- edge_mid: float32 [2, 128, 128], replicated, may hold values from -0.5 to 0.5
- edge_bias: float32 [3, 128], replicated, may hold values from -3 to 3
- node_in: float32 [256, 128], replicated, may hold values from -0.375 to 0.375
- node_mid: float32 [2, 128, 128], replicated, may hold values from -0.5 to 0.5
- node_bias: float32 [3, 128], replicated, may hold values from -3 to 3
Outputs:
- new_feat: float32 [131072, 128], P('dom')
- feat_grad: float32 [131072, 128], P('dom')
- edge_in_grad: float32 [256, 128], replicated
- edge_mid_grad: float32 [2, 128, 128], replicated
- edge_bias_grad: float32 [3, 128], replicated
- node_in_grad: float32 [256, 128], replicated
- node_mid_grad: float32 [2, 128, 128], replicated
- node_bias_grad: float32 [3, 128], replicated
Inputs may be any that keep to these rules, and one draw needn't show every extreme that they name: `lattice_of`: row s lists, for node k of element slot s, its lattice point x * 8 * 8 + y * 8 + z; every row is a permutation. `element_place`: row d lists, for each element slot of partition d, its place p in the partition's 2 x 2 x 2 block of elements, at offset (p // 4, p // 2 % 2, p % 2) in elements; every row is a permutation.
All inputs are finite; a program needn't handle non-finite values.
Results may differ from a plain program's by a relative error of at most 0.0003.
Values sent between devices are 32-bit elements; how exact they have to be, the bound alone decides.
A program may use at most 128 MiB of HBM per device.

v0:
```python
import math

import jax
import jax.numpy as jnp
from jax import lax
from jax.sharding import PartitionSpec as P

SIDE = 8
ELEM_DEV = 8
DGX = 4
DGY = 4
NODES_EL = 512


highest = lax.Precision.HIGHEST


def shifted(block, axis, distance):
    devices = range(lax.axis_size(axis))
    route = [(i - distance, i) for i in devices if i - distance in devices]
    return lax.ppermute(block, axis, route)


def matmul(values, weight):
    flat = values.reshape(-1, values.shape[-1])
    result = jnp.dot(flat, weight, precision=highest, preferred_element_type=jnp.float32)
    return result.reshape(values.shape[:-1] + (weight.shape[1],))


def edge_messages(lattice, edge_in, edge_mid, edge_bias):
    channels = lattice.shape[-1]
    extent = lattice.shape[1]
    toward = matmul(lattice, edge_in[:channels])
    source = matmul(lattice, edge_in[channels:])
    summed = jnp.zeros_like(lattice)
    for spatial in (1, 2, 3):
        for upward in (True, False):
            if upward:
                target = lax.slice_in_dim(toward, 0, extent - 1, axis=spatial)
                anchor = lax.slice_in_dim(source, 1, extent, axis=spatial)
                padding = (0, 1)
            else:
                target = lax.slice_in_dim(toward, 1, extent, axis=spatial)
                anchor = lax.slice_in_dim(source, 0, extent - 1, axis=spatial)
                padding = (1, 0)
            hidden = jax.nn.silu(target + anchor + edge_bias[0])
            hidden = jax.nn.silu(matmul(hidden, edge_mid[0]) + edge_bias[1])
            message = matmul(hidden, edge_mid[1]) + edge_bias[2]
            widths = [(0, 0)] * 5
            widths[spatial] = padding
            summed = summed + jnp.pad(message, widths)
    return summed


def node_update(lattice, gathered, node_in, node_mid, node_bias):
    channels = lattice.shape[-1]
    hidden = jax.nn.silu(
        matmul(lattice, node_in[:channels]) + matmul(gathered, node_in[channels:]) + node_bias[0]
    )
    hidden = jax.nn.silu(matmul(hidden, node_mid[0]) + node_bias[1])
    return lattice + matmul(hidden, node_mid[1]) + node_bias[2]


def to_lattice(node_rows, lattice_of):
    channels = node_rows.shape[-1]
    count = lattice_of.shape[0]
    blocks = node_rows.reshape(count, -1, channels)
    placed = jax.vmap(lambda values, ordering: jnp.zeros_like(values).at[ordering].set(values))(
        blocks, lattice_of
    )
    return placed.reshape(count, SIDE, SIDE, SIDE, channels)


def from_lattice(lattice, lattice_of):
    channels = lattice.shape[-1]
    count = lattice_of.shape[0]
    blocks = lattice.reshape(count, -1, channels)
    picked = jax.vmap(lambda values, ordering: values[ordering])(blocks, lattice_of)
    return picked.reshape(-1, channels)


def select(subset, level):
    return tuple((level if spatial in subset else slice(None) for spatial in range(3)))


def exchange_faces(field):
    devices = lax.axis_size("dom")
    index = lax.axis_index("dom")
    depth = devices // (DGX * DGY)
    grid = (index % DGX, index // DGX % DGY, index // (DGX * DGY))
    limits = (DGX, DGY, depth)
    strides = (1, DGX, DGX * DGY)
    has_lower = [grid[spatial] > 0 for spatial in range(3)]
    has_upper = [grid[spatial] < limits[spatial] - 1 for spatial in range(3)]
    extent = field.shape[0]
    last = extent - 1
    for spatial in (2, 1, 0):
        low_region = select((spatial,), 0)
        high_region = select((spatial,), last)
        low_plane = field[low_region]
        high_plane = field[high_region]
        from_above = shifted(low_plane, "dom", -strides[spatial])
        from_below = shifted(high_plane, "dom", strides[spatial])
        field = field.at[high_region].add(jnp.where(has_upper[spatial], from_above, 0.0))
        field = field.at[low_region].add(jnp.where(has_lower[spatial], from_below, 0.0))
    return field


def make_consistent(summed, placement):
    channels = summed.shape[-1]
    extent = 2 * SIDE - 1
    stride = SIDE - 1
    zero_index = jnp.zeros((), jnp.int32)
    sizes = (SIDE, SIDE, SIDE, channels)
    field = jnp.zeros((extent, extent, extent, channels), jnp.float32)
    starts = []
    for slot in range(summed.shape[0]):
        offset = placement[slot]
        start = (offset // 4 * stride, offset // 2 % 2 * stride, offset % 2 * stride, zero_index)
        starts.append(start)
        current = lax.dynamic_slice(field, start, sizes)
        field = lax.dynamic_update_slice(field, current + summed[slot], start)
    field = exchange_faces(field)
    return jnp.stack([lax.dynamic_slice(field, start, sizes) for start in starts])


def body(
    node_feat,
    out_grad,
    lattice_of,
    element_place,
    edge_in,
    edge_mid,
    edge_bias,
    node_in,
    node_mid,
    node_bias,
):
    lattice = to_lattice(node_feat, lattice_of)
    summed, edge_pullback = jax.vjp(edge_messages, lattice, edge_in, edge_mid, edge_bias)
    gathered = make_consistent(summed, element_place[0])
    updated, node_pullback = jax.vjp(node_update, lattice, gathered, node_in, node_mid, node_bias)
    cotangent = to_lattice(out_grad, lattice_of)
    direct_grad, around_grad, node_in_grad, node_mid_grad, node_bias_grad = node_pullback(cotangent)
    around_total = make_consistent(around_grad, element_place[0])
    edge_grad, edge_in_grad, edge_mid_grad, edge_bias_grad = edge_pullback(around_total)
    totals = lax.psum(
        (edge_in_grad, edge_mid_grad, edge_bias_grad, node_in_grad, node_mid_grad, node_bias_grad),
        "dom",
    )
    scale = 1.0 / math.sqrt(lax.axis_size("dom") * ELEM_DEV * NODES_EL)
    new_feat = from_lattice(updated, lattice_of)
    feat_grad = from_lattice(direct_grad + edge_grad, lattice_of)
    return (new_feat, feat_grad) + tuple((entry * scale for entry in totals))


def solution(mesh):
    in_specs = (
        P("dom", None),
        P("dom", None),
        P("dom", None),
        P("dom", None),
        P(),
        P(),
        P(),
        P(),
        P(),
        P(),
    )
    out_specs = (P("dom", None), P("dom", None), P(), P(), P(), P(), P(), P())
    return jax.shard_map(body, mesh=mesh, in_specs=in_specs, out_specs=out_specs, check_vma=False)
```

profile of v0, /device:TPU:0, one launch (start us, length us, event | category | flops | bytes accessed | tf_op | source)
XLA Modules:
  0.0 551.2 jit_solution(3502911191136592071)
XLA Ops:
  32.2 11.6 %scatter_custom_fusion = f32[4096,128]{1,0:T(8,128)S(1)} fusion(s32[4096]{0:T(1024)S(1)} %bitcast.464, f32[4096,128]{1,0:T(8,128)} %param.34, f32[]{:T(128)} %constant.608.clone.1), kind=kCustom, calls=%fused_computation.141 | custom fusion | bytes 2097664 | tf_op jit(solution)/shard_map/jvp()/reshape;reshape | solution.py:25
  112.7 9.8 %collective-permute-done = f32[15,15,128]{2,0,1:T(8,128)S(1)} collective-permute-done((f32[15,15,128]{2,0,1:T(8,128)S(1)}, f32[15,15,128]{2,0,1:T(8,128)S(1)}, u32[]{:S(2)}, u32[]{:S(2)}) %collective-permute-start) | collective-permute-done | bytes 115232 | tf_op jit(solution)/shard_map/ppermute | solution.py:21
  130.2 5.7 %collective-permute-done.2 = f32[15,15,128]{2,1,0:T(8,128)S(1)} collective-permute-done((f32[15,15,128]{2,1,0:T(8,128)S(1)}, f32[15,15,128]{2,1,0:T(8,128)S(1)}, u32[]{:S(2)}, u32[]{:S(2)}) %collective-permute-start.2) | collective-permute-done | bytes 115232 | tf_op jit(solution)/shard_map/ppermute | solution.py:21
  135.9 4.8 collective-permute-start.3
  143.9 4.1 scatter-add.44
  149.5 4.1 scatter-add.45
  155.9 11.4 %scatter_custom_fusion.1 = f32[4096,128]{1,0:T(8,128)S(1)} fusion(s32[4096]{0:T(1024)S(1)} %bitcast.465, f32[4096,128]{1,0:T(8,128)} %param.35, f32[]{:T(128)} %constant.608.clone.1), kind=kCustom, calls=%fused_computation.139 | custom fusion | bytes 2097664 | tf_op jit(solution)/shard_map/transpose(jvp())/reshape;reshape | solution.py:27
  188.1 3.8 convolution_bitcast_fusion
  194.4 4.2 convolution_bitcast_fusion.2
  212.7 4.2 add_add_fusion.1
  216.8 7.9 %collective-permute-done.6 = f32[15,15,128]{2,0,1:T(8,128)S(1)} collective-permute-done((f32[15,15,128]{2,0,1:T(8,128)S(1)}, f32[15,15,128]{2,0,1:T(8,128)S(1)}, u32[]{:S(2)}, u32[]{:S(2)}) %collective-permute-start.6) | collective-permute-done | bytes 115232 | tf_op jit(solution)/shard_map/ppermute | solution.py:21
  232.9 4.2 scatter-add.51
  239.6 4.8 fusion.128
  246.6 3.8 collective-permute-start.9
  254.0 44.8 %gather_fusion = f32[4096,128]{1,0:T(8,128)} fusion(f32[8,512,128]{2,1,0:T(8,128)S(1)} %bitcast.441, s32[4096]{0:T(1024)S(1)} %bitcast.438), kind=kCustom, calls=%fused_computation | custom fusion | bytes 4227072 | tf_op jit(solution)/shard_map/vmap()/gather | solution.py:78
  307.7 3.8 collective-permute-start.11
  326.8 4.4 fusion.84
  334.5 4.7 convolution_bitcast_fusion.6
  342.6 4.0 fusion.87
  349.9 4.5 convolution_bitcast_fusion.5
  374.9 3.6 convolution_bitcast_fusion.4
  408.9 44.8 %gather_fusion.1 = f32[4096,128]{1,0:T(8,128)} fusion(f32[8,512,128]{2,1,0:T(8,128)S(1)} %bitcast.440, s32[4096]{0:T(1024)S(1)} %bitcast.439), kind=kCustom, calls=%fused_computation.1 | custom fusion | bytes 4227072 | tf_op jit(solution)/shard_map/vmap()/gather | solution.py:78
  453.6 44.2 %all-reduce.57 = (f32[3,128]{1,0:T(4,128)S(1)}, f32[3,128]{1,0:T(4,128)S(1)}) all-reduce(f32[3,128]{1,0:T(4,128)S(1)} %pad_add_fusion.9, f32[3,128]{1,0:T(4,128)S(1)} %pad_add_fusion.8), channel_id=1, replica_groups=mesh['dom'=32] {'dom'}, use_global_device_ids=true, to_apply=%region_22.23 | all-reduce | flops 768 | bytes 6144 | tf_op jit(solution)/shard_map/psum | solution.py:147
  498.4 42.4 %all-reduce.61.cloned.1.call-done = (f32[256,128]{1,0:T(8,128)}, f32[2,128,128]{2,1,0:T(8,128)}, f32[256,128]{1,0:T(8,128)}, f32[2,128,128]{2,1,0:T(8,128)}) async-done(((f32[256,128]{1,0:T(8,128)}, f32[2,128,128]{2,1,0:T(8,128)}, f32[256,128]{1,0:T(8,128)}, f32[2,128,128]{2,1,0:T(8,128)}), (f32[256,128]{1,0:T(8,128)}, f32[2,128,128]{2,1,0:T(8,128)}, f32[256,128]{1,0:T(8,128)}, ...) | async-done | bytes 524304 | tf_op jit(solution)/shard_map/psum | solution.py:147
  (266 shorter events, 229.0 us)
Async XLA Ops:
  7.2 36.6 %copy-start.20 = (f32[256,128]{1,0:T(8,128)S(1)}, f32[256,128]{1,0:T(8,128)}, u32[]{:S(2)}) copy-start(f32[256,128]{1,0:T(8,128)} %param.38) | copy-start | bytes 393220
  7.2 533.6 %all-reduce.61.cloned.1.call-start = ((), (), s32[]{:S(2)}) async-start(), calls=%async_computation | async-start | bytes 1048576 | tf_op jit(solution)/shard_map/psum | solution.py:147
  43.8 96.9 %copy-start = (f32[4096,128]{1,0:T(8,128)}, f32[4096,128]{1,0:T(8,128)S(1)}, u32[]{:S(2)}) copy-start(f32[4096,128]{1,0:T(8,128)S(1)} %scatter_custom_fusion) | copy-start | bytes 6291460
  49.6 18.2 %copy-start.30 = (f32[8,8,8,7,128]{4,2,3,1,0:T(8,128)}, f32[8,8,8,7,128]{4,2,3,1,0:T(8,128)S(1)}, u32[]{:S(2)}) copy-start(f32[8,8,8,7,128]{4,2,3,1,0:T(8,128)S(1)} %fusion.154) | copy-start | bytes 5505028
  51.5 14.4 %copy-start.34 = (f32[8,8,8,7,128]{4,2,3,1,0:T(8,128)}, f32[8,8,8,7,128]{4,2,3,1,0:T(8,128)S(1)}, u32[]{:S(2)}) copy-start(f32[8,8,8,7,128]{4,2,3,1,0:T(8,128)S(1)} %fusion.156) | copy-start | bytes 5505028
  59.0 14.0 %copy-start.40 = (f32[8,8,7,8,128]{4,2,3,1,0:T(8,128)}, f32[8,8,7,8,128]{4,2,3,1,0:T(8,128)S(1)}, u32[]{:S(2)}) copy-start(f32[8,8,7,8,128]{4,2,3,1,0:T(8,128)S(1)} %fusion.158) | copy-start | bytes 5505028
  108.4 32.3 %copy-start.18 = (f32[256,128]{1,0:T(8,128)S(1)}, f32[256,128]{1,0:T(8,128)}, u32[]{:S(2)}) copy-start(f32[256,128]{1,0:T(8,128)} %param.41) | copy-start | bytes 393220
  111.4 11.1 %collective-permute-start = (f32[15,15,128]{2,0,1:T(8,128)S(1)}, f32[15,15,128]{2,0,1:T(8,128)S(1)}, u32[]{:S(2)}, u32[]{:S(2)}) collective-permute-start(f32[15,15,128]{2,0,1:T(8,128)S(1)} %bitcast.462), channel_id=1, source_target_pairs={{16,0},{17,1},{18,2},{19,3},{20,4},{21,5},{22,6},{23,7},{24,8},{25... | collective-permute-start | bytes 345608 | tf_op jit(solution)/shard_map/ppermute | solution.py:21
  122.5 3.9 collective-permute-start.1
  128.8 7.0 %collective-permute-start.2 = (f32[15,15,128]{2,1,0:T(8,128)S(1)}, f32[15,15,128]{2,1,0:T(8,128)S(1)}, u32[]{:S(2)}, u32[]{:S(2)}) collective-permute-start(f32[15,15,128]{2,1,0:T(8,128)S(1)} %bitcast.463), channel_id=1, source_target_pairs={{4,0},{5,1},{6,2},{7,3},{8,4},{9,5},{10,6},{11,7},{12,8},{13,9},{1... | collective-permute-start | bytes 345608 | tf_op jit(solution)/shard_map/ppermute | solution.py:21
  135.9 20.0 %copy-start.22 = (s32[8,512]{1,0:T(8,128)S(1)}, s32[8,512]{1,0:T(8,128)}, u32[]{:S(2)}) copy-start(s32[8,512]{1,0:T(8,128)} %param.36) | copy-start | bytes 49156
  135.9 13.4 %collective-permute-start.3 = (f32[15,15,128]{2,1,0:T(8,128)S(1)}, f32[15,15,128]{2,1,0:T(8,128)S(1)}, u32[]{:S(2)}, u32[]{:S(2)}) collective-permute-start(f32[15,15,128]{2,1,0:T(8,128)S(1)} %get-tuple-element.203), channel_id=1, source_target_pairs={{0,4},{1,5},{2,6},{3,7},{4,8},{5,9},{6,10},{7,11},{8,12},{9,13},{1... | collective-permute-start | bytes 345608 | tf_op jit(solution)/shard_map/ppermute | solution.py:21
  154.5 13.3 %collective-permute-start.4 = (f32[15,15,128]{2,0,1:T(8,128)S(1)}, f32[15,15,128]{2,0,1:T(8,128)S(1)}, u32[]{:S(2)}, u32[]{:S(2)}) collective-permute-start(f32[15,15,128]{2,0,1:T(8,128)S(1)} %slice_bitcast_fusion.4), channel_id=1, source_target_pairs={{1,0},{2,1},{3,2},{4,3},{5,4},{6,5},{7,6},{8,7},{9,8},{10,9},{11,1... | collective-permute-start | bytes 345608 | tf_op jit(solution)/shard_map/ppermute | solution.py:21
  155.9 17.2 %copy-start.27 = (f32[3,128]{1,0:T(4,128)S(1)}, f32[3,128]{1,0:T(4,128)}, u32[]{:S(2)}) copy-start(f32[3,128]{1,0:T(4,128)} %param.43) | copy-start | bytes 4612
  167.3 18.3 %copy-start.3 = (f32[4096,128]{1,0:T(8,128)}, f32[4096,128]{1,0:T(8,128)S(1)}, u32[]{:S(2)}) copy-start(f32[4096,128]{1,0:T(8,128)S(1)} %scatter_custom_fusion.1) | copy-start | bytes 6291460
  169.6 4.0 collective-permute-start.5
  211.3 13.4 %collective-permute-start.6 = (f32[15,15,128]{2,0,1:T(8,128)S(1)}, f32[15,15,128]{2,0,1:T(8,128)S(1)}, u32[]{:S(2)}, u32[]{:S(2)}) collective-permute-start(f32[15,15,128]{2,0,1:T(8,128)S(1)} %slice_bitcast_fusion.3), channel_id=1, source_target_pairs={{16,0},{17,1},{18,2},{19,3},{20,4},{21,5},{22,6},{23,7},{24,8},{25... | collective-permute-start | bytes 345608 | tf_op jit(solution)/shard_map/ppermute | solution.py:21
  212.6 14.6 %copy-start.1 = (f32[4096,128]{1,0:T(8,128)S(1)}, f32[4096,128]{1,0:T(8,128)}, u32[]{:S(2)}) copy-start(f32[4096,128]{1,0:T(8,128)} %copy-done) | copy-start | bytes 6291460
  212.6 14.6 %copy-start.7 = (f32[8,8,8,8,128]{4,3,2,1,0:T(8,128)S(1)}, f32[8,8,8,8,128]{4,3,2,1,0:T(8,128)}, u32[]{:S(2)}) copy-start(f32[8,8,8,8,128]{4,3,2,1,0:T(8,128)} %copy-done.6) | copy-start | bytes 6291460
  224.7 8.0 %collective-permute-start.7 = (f32[15,15,128]{2,0,1:T(8,128)S(1)}, f32[15,15,128]{2,0,1:T(8,128)S(1)}, u32[]{:S(2)}, u32[]{:S(2)}) collective-permute-start(f32[15,15,128]{2,0,1:T(8,128)S(1)} %get-tuple-element.185), channel_id=1, source_target_pairs={{0,16},{1,17},{2,18},{3,19},{4,20},{5,21},{6,22},{7,23},{8,24},{9,... | collective-permute-start | bytes 345608 | tf_op jit(solution)/shard_map/ppermute | solution.py:21
  238.0 7.0 %collective-permute-start.8 = (f32[15,15,128]{2,1,0:T(8,128)S(1)}, f32[15,15,128]{2,1,0:T(8,128)S(1)}, u32[]{:S(2)}, u32[]{:S(2)}) collective-permute-start(f32[15,15,128]{2,1,0:T(8,128)S(1)} %slice_bitcast_fusion.2), channel_id=1, source_target_pairs={{4,0},{5,1},{6,2},{7,3},{8,4},{9,5},{10,6},{11,7},{12,8},{13,9},{1... | collective-permute-start | bytes 345608 | tf_op jit(solution)/shard_map/ppermute | solution.py:21
  246.6 55.3 %collective-permute-start.9 = (f32[15,15,128]{2,1,0:T(8,128)S(1)}, f32[15,15,128]{2,1,0:T(8,128)S(1)}, u32[]{:S(2)}, u32[]{:S(2)}) collective-permute-start(f32[15,15,128]{2,1,0:T(8,128)S(1)} %get-tuple-element.183), channel_id=1, source_target_pairs={{0,4},{1,5},{2,6},{3,7},{4,8},{5,9},{6,10},{7,11},{8,12},{9,13},{1... | collective-permute-start | bytes 345608 | tf_op jit(solution)/shard_map/ppermute | solution.py:21
  304.4 3.2 collective-permute-start.10
  307.7 4.6 collective-permute-start.11
  (31 other events, 152.7 us)
Sparse Core Ops, SparseCore 0:
  408.9 131.7 all-reduce.60
where the time goes:
time: 556 us; the launch traced here: 551 us
  local copies, waits for them, and re-layouts  181 us (33%)
  matrix products  159 us (29%)
  waiting for transfers between devices  69.1 us (12%)
  blocking collectives  44.2 us (8%)
  between operations  36.8 us (7%)
  other arithmetic  33.6 us (6%)
  starting transfers between devices  27.9 us (5%)
    dot_general x54, matrix products, matmul(): jnp.dot(flat, weight, precision=highest, preferred_element_type=jnp.float32)  159 us
    gather x2, local copies, waits for them, and re-layouts, from_lattice(): values[ordering]  89.6 us
    psum x1, blocking collectives, body(): lax.psum((edge_in_grad, edge_mid_grad, edge_bias_grad, node_in_grad, node...  44.2 us
    psum x1, waiting for transfers between devices, body(): lax.psum((edge_in_grad, edge_mid_grad, edge_bias_grad, node_in_grad, node...  42.4 us
    ppermute x12, starting transfers between devices, shifted(): return lax.ppermute(block, axis, route)  27.8 us
    ppermute x12, waiting for transfers between devices, shifted(): return lax.ppermute(block, axis, route)  26.7 us
    dynamic_update_slice x17, local copies, waits for them, and re-layouts, make_consistent(): field = lax.dynamic_update_slice(field, current + summed[slot], start)  24 us
    add x14, other arithmetic, make_consistent(): field = lax.dynamic_update_slice(field, current + summed[slot], start)  13.6 us
  transfers between devices with their start and end apart: 13, of which 9 were waited for; matrix products, arithmetic and copies ran while one was open for 24% of the time, Pallas kernels for 0%

commit v1 on v0

v1 whole, which is shorter than its diff:
```python
import functools
import math

import jax
import jax.numpy as jnp
from jax import lax
from jax.experimental import pallas as pl
from jax.experimental.pallas import tpu as pltpu
from jax.sharding import PartitionSpec as P

SIDE = 8
ELEM_DEV = 8
DGX = 4
DGY = 4
NODES_EL = 512

F32 = jnp.float32
BF16 = jnp.bfloat16
VMEM_BYTES = 48 * 2**20
PAIRS = ((2, True), (2, False), (0, True), (0, False), (1, True), (1, False))


def split(values):
    high = values.astype(BF16)
    low = (values - high.astype(F32)).astype(BF16)
    return jnp.concatenate([high, low], axis=1)


def spread(weight):
    halves = split(weight)
    return jnp.concatenate([halves, halves], axis=0)


def times(pair, spread_weight):
    wide = jnp.dot(pair, spread_weight, preferred_element_type=F32)
    half = wide.shape[1] // 2
    return wide[:, :half] + wide[:, half:]


def across(left, right):
    wide = lax.dot_general(left, right, (((0,), (0,)), ((), ())), preferred_element_type=F32)
    m, n = wide.shape[0] // 2, wide.shape[1] // 2
    return (wide[:m, :n] + wide[m:, n:]) + (wide[:m, n:] + wide[m:, :n])


def column_sum(values):
    return jnp.sum(values, axis=0, keepdims=True)


def one_hot(order):
    n = order.shape[1]
    points = lax.broadcasted_iota(jnp.int32, (n, n), 0)
    return jnp.where(points == order, 1.0, 0.0).astype(BF16)


def place_rows(hot, values):
    wide = jnp.dot(hot, split(values), preferred_element_type=F32)
    half = wide.shape[1] // 2
    return wide[:, :half] + wide[:, half:]


def pick_rows(hot, values):
    wide = lax.dot_general(hot, split(values), (((0,), (0,)), ((), ())), preferred_element_type=F32)
    half = wide.shape[1] // 2
    return wide[:, :half] + wide[:, half:]


def slope(half_value, tanh):
    return (1.0 + tanh) * (1.0 + half_value * (1.0 - tanh))


def window(axis, first):
    index = [slice(None)] * 3
    if axis != 2:
        index[axis] = slice(0, SIDE - 1) if first else slice(1, SIDE)
    return tuple(index)


def rows_of(ref, axis, first):
    picked = ref[window(axis, first)]
    return picked.reshape(-1, picked.shape[-1])


def rolled(rows, shift):
    grouped = rows.reshape(-1, SIDE, rows.shape[-1])
    return pltpu.roll(grouped, shift % SIDE, 1).reshape(rows.shape)


def add_rows(ref, axis, first, rows):
    index = window(axis, first)
    ref[index] += rows.reshape(ref[index].shape)


def inner(rows, channels, upward):
    z = lax.broadcasted_iota(jnp.int32, (rows, channels), 0) % SIDE
    return z < SIDE - 1 if upward else z > 0


def degree(rows, channels):
    at = lax.broadcasted_iota(jnp.int32, (rows, channels), 0)
    total = jnp.zeros((rows, channels), F32)
    for coordinate in (at // (SIDE * SIDE), at // SIDE % SIDE, at % SIDE):
        edge = (coordinate == 0) | (coordinate == SIDE - 1)
        total = total + jnp.where(edge, 1.0, 2.0)
    return total


def senders(source, axis, upward):
    if axis == 2:
        whole = source[...].reshape(-1, source.shape[-1])
        return rolled(whole, -1 if upward else 1)
    return rows_of(source, axis, not upward)


def edge_forward_kernel(
    place, feat, order, w_in, w_mid, bias,
    lattice_out, summed_out, local_out,
    toward, source, total, w_toward, w_source, w_hidden, w_last,
):
    channels = feat.shape[1]

    @pl.when(pl.program_id(0) == 0)
    def _():
        w_toward[...] = spread(0.5 * w_in[:channels])
        w_source[...] = spread(0.5 * w_in[channels:])
        w_hidden[...] = spread(0.5 * w_mid[0])
        w_last[...] = spread(w_mid[1])

    lattice = place_rows(one_hot(order[0]), feat[...])
    lattice_out[...] = lattice
    pair = split(lattice)
    shape = toward.shape
    toward[...] = (times(pair, w_toward[...]) + 0.5 * bias[0:1]).reshape(shape)
    source[...] = times(pair, w_source[...]).reshape(shape)
    bias_half = 0.5 * bias[1:2]
    for axis, upward in PAIRS:
        y = rows_of(toward, axis, upward) + senders(source, axis, upward)
        hidden = y + y * jnp.tanh(y)
        y = times(split(hidden), w_hidden[...]) + bias_half
        hidden = y + y * jnp.tanh(y)
        if axis == 2:
            hidden = jnp.where(inner(*hidden.shape, upward), hidden, 0.0)
        if (axis, upward) == PAIRS[0]:
            total[...] = hidden.reshape(shape)
        else:
            add_rows(total, axis, upward, hidden)
    summed = total[...].reshape(lattice.shape)
    summed_out[...] = summed
    local_out[...] = times(split(summed), w_last[...]) + degree(*lattice.shape) * bias[2:3]


def node_kernel(
    place, lattice_ref, gathered_ref, cotangent, order, w_in, w_mid, bias,
    new_out, direct_out, around_out, grads,
    w_own, w_near, w_hidden, w_last, b_own, b_near, b_hidden, b_last,
):
    channels = lattice_ref.shape[1]

    @pl.when(pl.program_id(0) == 0)
    def _():
        w_own[...] = spread(0.5 * w_in[:channels])
        w_near[...] = spread(0.5 * w_in[channels:])
        w_hidden[...] = spread(0.5 * w_mid[0])
        w_last[...] = spread(w_mid[1])
        b_own[...] = spread(w_in[:channels].T)
        b_near[...] = spread(w_in[channels:].T)
        b_hidden[...] = spread(0.5 * w_mid[0].T)
        b_last[...] = spread(0.5 * w_mid[1].T)
        grads[...] = jnp.zeros(grads.shape, F32)

    hot = one_hot(order[0])
    lattice = lattice_ref[...]
    own = split(lattice)
    near = split(gathered_ref[...])
    y1 = times(own, w_own[...]) + times(near, w_near[...]) + 0.5 * bias[0:1]
    t1 = jnp.tanh(y1)
    hidden1 = split(y1 + y1 * t1)
    y2 = times(hidden1, w_hidden[...]) + 0.5 * bias[1:2]
    t2 = jnp.tanh(y2)
    hidden2 = split(y2 + y2 * t2)
    new_out[...] = pick_rows(hot, lattice + times(hidden2, w_last[...]) + bias[2:3])

    incoming = place_rows(hot, cotangent[...])
    incoming_pair = split(incoming)
    back2 = times(incoming_pair, b_last[...]) * slope(y2, t2)
    back2_pair = split(back2)
    back1 = times(back2_pair, b_hidden[...]) * slope(y1, t1)
    back1_pair = split(back1)
    direct_out[...] = incoming + times(back1_pair, b_own[...])
    around_out[...] = times(back1_pair, b_near[...])
    c = channels
    grads[0:c] += across(own, back1_pair)
    grads[c:2 * c] += across(near, back1_pair)
    grads[2 * c:3 * c] += across(hidden1, back2_pair)
    grads[3 * c:4 * c] += across(hidden2, incoming_pair)
    grads[4 * c:4 * c + 1] += column_sum(back1)
    grads[4 * c + 1:4 * c + 2] += column_sum(back2)
    grads[4 * c + 2:4 * c + 3] += column_sum(incoming)


def edge_backward_kernel(
    place, lattice_ref, around_ref, summed_ref, direct_ref, order, w_in, w_mid, bias,
    feat_out, grads,
    toward, source, incoming, to_toward, to_source, left, right,
    w_toward, w_source, w_hidden, b_toward, b_source, b_hidden, b_last,
):
    channels = lattice_ref.shape[1]
    c = channels

    @pl.when(pl.program_id(0) == 0)
    def _():
        w_toward[...] = spread(0.5 * w_in[:channels])
        w_source[...] = spread(0.5 * w_in[channels:])
        w_hidden[...] = spread(0.5 * w_mid[0])
        b_toward[...] = spread(w_in[:channels].T)
        b_source[...] = spread(w_in[channels:].T)
        b_hidden[...] = spread(0.5 * w_mid[0].T)
        b_last[...] = spread(0.5 * w_mid[1].T)
        grads[...] = jnp.zeros(grads.shape, F32)

    around = around_ref[...]
    around_pair = split(around)
    shape = toward.shape
    pair = split(lattice_ref[...])
    toward[...] = (times(pair, w_toward[...]) + 0.5 * bias[0:1]).reshape(shape)
    source[...] = times(pair, w_source[...]).reshape(shape)
    incoming[...] = times(around_pair, b_last[...]).reshape(shape)
    bias_half = 0.5 * bias[1:2]
    back2_sum = jnp.zeros((1, channels), F32)
    start = 0
    for axis, upward in PAIRS:
        y1 = rows_of(toward, axis, upward) + senders(source, axis, upward)
        rows = y1.shape[0]
        span = slice(start, start + rows)
        start += rows
        t1 = jnp.tanh(y1)
        hidden_pair = split(y1 + y1 * t1)
        left[span] = hidden_pair
        y2 = times(hidden_pair, w_hidden[...]) + bias_half
        t2 = jnp.tanh(y2)
        arrived = rows_of(incoming, axis, upward)
        if axis == 2:
            arrived = jnp.where(inner(*arrived.shape, upward), arrived, 0.0)
        back2 = arrived * slope(y2, t2)
        back2_sum = back2_sum + column_sum(back2)
        back2_pair = split(back2)
        right[span] = back2_pair
        back1 = times(back2_pair, b_hidden[...]) * slope(y1, t1)
        sent = rolled(back1, 1 if upward else -1) if axis == 2 else back1
        if (axis, upward) == PAIRS[0]:
            to_toward[...] = back1.reshape(shape)
            to_source[...] = sent.reshape(shape)
        else:
            add_rows(to_toward, axis, upward, back1)
            add_rows(to_source, axis, not upward, sent)
    back_toward = to_toward[...].reshape(around.shape)
    toward_pair = split(back_toward)
    source_pair = split(to_source[...].reshape(around.shape))
    total = direct_ref[...] + times(toward_pair, b_toward[...]) + times(source_pair, b_source[...])
    feat_out[...] = pick_rows(one_hot(order[0]), total)
    grads[0:c] += across(pair, toward_pair)
    grads[c:2 * c] += across(pair, source_pair)
    grads[2 * c:3 * c] += across(left[...], right[...])
    grads[3 * c:4 * c] += across(split(summed_ref[...]), around_pair)
    grads[4 * c:4 * c + 1] += column_sum(back_toward)
    grads[4 * c + 1:4 * c + 2] += back2_sum
    grads[4 * c + 2:4 * c + 3] += column_sum(around * degree(*around.shape))


def slot_at(place, at):
    slot = jnp.int32(0)
    for s in range(ELEM_DEV):
        slot = slot + jnp.where(place[0, s] == at, jnp.int32(s), jnp.int32(0))
    return slot


def on_elements(kernel, place, arrays, slotted, weights, order, out_rows, out_slotted, grads, scratch, cost):
    channels = arrays[0].shape[1]
    by_slot = pl.BlockSpec((NODES_EL, channels), lambda p, place: (slot_at(place, p), 0))
    by_place = pl.BlockSpec((NODES_EL, channels), lambda p, place: (p, 0))

    def whole(array):
        zeros = (0,) * array.ndim
        return pl.BlockSpec(array.shape, lambda p, place: zeros)

    order3 = order.reshape(order.shape[0], 1, order.shape[1])
    in_specs = [by_slot if s else by_place for s in slotted]
    in_specs.append(pl.BlockSpec((1, 1, order.shape[1]), lambda p, place: (slot_at(place, p), 0, 0)))
    in_specs += [whole(w) for w in weights]
    rows = order.shape[0] * NODES_EL
    out_shape = [jax.ShapeDtypeStruct((rows, channels), F32) for _ in range(out_rows)]
    out_specs = [by_slot if s else by_place for s in out_slotted]
    if grads:
        total = jax.ShapeDtypeStruct((4 * channels + SIDE, channels), F32)
        out_shape.append(total)
        out_specs.append(whole(total))
    return pl.pallas_call(
        kernel,
        grid_spec=pltpu.PrefetchScalarGridSpec(
            num_scalar_prefetch=1,
            grid=(order.shape[0],),
            in_specs=in_specs,
            out_specs=out_specs,
            scratch_shapes=scratch,
        ),
        out_shape=out_shape,
        cost_estimate=cost,
        compiler_params=pltpu.CompilerParams(
            dimension_semantics=("arbitrary",), vmem_limit_bytes=VMEM_BYTES
        ),
    )(place, *arrays, order3, *weights)


def plane(axis, element, side):
    base = element * NODES_EL
    far = (SIDE - 1) * side
    if axis == 0:
        return [(pl.ds(base + far * SIDE * SIDE, SIDE * SIDE), SIDE * SIDE)]
    if axis == 1:
        return [(pl.ds(base + x * SIDE * SIDE + far * SIDE, SIDE), SIDE) for x in range(SIDE)]
    return [(pl.ds(base + far, SIDE * SIDE, stride=SIDE), SIDE * SIDE)]


def exchange_kernel(devices, field_in, field, outgoing, arriving, send_sem, recv_sem):
    me = lax.axis_index("dom")
    depth = devices // (DGX * DGY)
    grid = (me % DGX, me // DGX % DGY, me // (DGX * DGY))
    limits = (DGX, DGY, depth)
    strides = (1, DGX, DGX * DGY)
    exists = []
    partner = []
    for axis in range(3):
        exists.append((grid[axis] > 0, grid[axis] < limits[axis] - 1))
        partner.append(
            (
                jnp.where(exists[axis][0], me - strides[axis], me + strides[axis]),
                jnp.where(exists[axis][1], me + strides[axis], me - strides[axis]),
            )
        )
    barrier = pltpu.get_barrier_semaphore()
    for axis in range(3):
        for side in range(2):

            @pl.when(exists[axis][side])
            def _():
                pl.semaphore_signal(
                    barrier, inc=1, device_id=(partner[axis][side],), device_id_type=pl.DeviceIdType.MESH
                )

    field[...] = field_in[...]
    peers = jnp.int32(0)
    for axis in range(3):
        for side in range(2):
            peers = peers + jnp.where(exists[axis][side], jnp.int32(1), jnp.int32(0))
    pl.semaphore_wait(barrier, peers)
    for axis in (2, 1, 0):
        weight = (4, 2, 1)[axis]
        sides = [[p for p in range(ELEM_DEV) if p // weight % 2 == side] for side in range(2)]
        copies = []
        for side in range(2):
            at = 0
            for element in sides[side]:
                for rows, count in plane(axis, element, side):
                    outgoing[axis, side, at:at + count] = field[rows]
                    at += count
            copies.append(
                pltpu.make_async_remote_copy(
                    src_ref=outgoing.at[axis, side],
                    dst_ref=arriving.at[axis, 1 - side],
                    send_sem=send_sem.at[axis, side],
                    recv_sem=recv_sem.at[axis, 1 - side],
                    device_id=(partner[axis][side],),
                    device_id_type=pl.DeviceIdType.MESH,
                )
            )
        for side in range(2):

            @pl.when(exists[axis][side])
            def _():
                copies[side].start()

        for lower, upper in zip(*sides):
            for (rows_l, _), (rows_u, _) in zip(plane(axis, lower, 1), plane(axis, upper, 0)):
                both = field[rows_l] + field[rows_u]
                field[rows_l] = both
                field[rows_u] = both
        for side in range(2):

            @pl.when(exists[axis][side])
            def _():
                copies[1 - side].wait_recv()
                at = 0
                for element in sides[side]:
                    for rows, count in plane(axis, element, side):
                        field[rows] += arriving[axis, side, at:at + count]
                        at += count
                copies[side].wait_send()


def make_consistent(field, collective):
    devices = lax.axis_size("dom")
    face = ELEM_DEV // 2 * SIDE * SIDE
    channels = field.shape[1]
    return pl.pallas_call(
        functools.partial(exchange_kernel, devices),
        out_shape=jax.ShapeDtypeStruct(field.shape, F32),
        in_specs=[pl.BlockSpec(memory_space=pltpu.VMEM)],
        out_specs=pl.BlockSpec(memory_space=pltpu.VMEM),
        scratch_shapes=[
            pltpu.VMEM((3, 2, face, channels), F32),
            pltpu.VMEM((3, 2, face, channels), F32),
            pltpu.SemaphoreType.DMA((3, 2)),
            pltpu.SemaphoreType.DMA((3, 2)),
        ],
        compiler_params=pltpu.CompilerParams(
            collective_id=collective, has_side_effects=True, vmem_limit_bytes=VMEM_BYTES
        ),
    )(field)


def unpack(total, scale):
    channels = total.shape[1]
    c = channels
    total = total * scale
    return total[:2 * c], total[2 * c:4 * c].reshape(2, c, c), total[4 * c:4 * c + 3]


def body(
    node_feat,
    out_grad,
    lattice_of,
    element_place,
    edge_in,
    edge_mid,
    edge_bias,
    node_in,
    node_mid,
    node_bias,
):
    channels = node_feat.shape[1]
    cube = pltpu.VMEM((SIDE, SIDE, SIDE, channels), F32)
    wide = pltpu.VMEM((2 * channels, 2 * channels), BF16)
    pairs = 4 * (NODES_EL - SIDE * SIDE) + 2 * NODES_EL
    edge = (edge_in, edge_mid, edge_bias)
    node = (node_in, node_mid, node_bias)

    def cost(rows):
        return pl.CostEstimate(
            flops=8 * rows * channels * channels * lattice_of.shape[0],
            bytes_accessed=16 * node_feat.size,
            transcendentals=0,
        )

    lattice, summed, local = on_elements(
        edge_forward_kernel, element_place, [node_feat], [True], edge, lattice_of,
        3, [False] * 3, False, [cube] * 3 + [wide] * 4, cost(pairs),
    )
    gathered = make_consistent(local, 0)
    new_feat, direct, around, node_total = on_elements(
        node_kernel, element_place, [lattice, gathered, out_grad], [False, False, True], node, lattice_of,
        3, [True, False, False], True, [wide] * 8, cost(12 * NODES_EL),
    )
    around = make_consistent(around, 1)
    node_total = lax.psum(node_total, "dom")
    tall = pltpu.VMEM((pairs, 2 * channels), BF16)
    feat_grad, edge_total = on_elements(
        edge_backward_kernel, element_place, [lattice, around, summed, direct], [False] * 4, edge, lattice_of,
        1, [True], True, [cube] * 5 + [tall] * 2 + [wide] * 7, cost(3 * pairs),
    )
    edge_total = lax.psum(edge_total, "dom")
    scale = 1.0 / math.sqrt(lax.axis_size("dom") * ELEM_DEV * NODES_EL)
    return (new_feat, feat_grad) + unpack(edge_total, scale) + unpack(node_total, scale)


def solution(mesh):
    in_specs = (
        P("dom", None),
        P("dom", None),
        P("dom", None),
        P("dom", None),
        P(),
        P(),
        P(),
        P(),
        P(),
        P(),
    )
    out_specs = (P("dom", None), P("dom", None), P(), P(), P(), P(), P(), P())
    return jax.shard_map(body, mesh=mesh, in_specs=in_specs, out_specs=out_specs, check_vma=False)
```

time: 556 us -> 252 us (0.45)
  local copies, waits for them, and re-layouts: 181 us -> 13.4 us
  matrix products: 159 us -> 0 us
  Pallas kernels: 0 us -> 94.4 us
  waiting for transfers between devices: 69.1 us -> 128 us
  blocking collectives: 44.2 us -> 0 us
  other arithmetic: 33.6 us -> 1.08 us
  starting transfers between devices: 27.9 us -> 0.04 us
  between operations: 36.8 us -> 14.1 us
    dot_general x54 -> x0, matrix products: 159 us -> none  [matmul(): jnp.dot(flat, weight, precision=highest, preferred_element_type=jnp.float32)]
    pallas_call x0 -> x5, Pallas kernels: none -> 94.4 us  [the longest x3 58.3 us: on_elements(): pl.pallas_call(kernel, grid_spec=pltpu.PrefetchScalarGridSpec(num_scalar_...]
    gather x2 -> x0, local copies, waits for them, and re-layouts: 89.6 us -> none  [from_lattice(): values[ordering]]
    psum x1, waiting for transfers between devices: 42.4 us -> 128 us  [body(): edge_total = lax.psum(edge_total, 'dom')]
    psum x1 -> x0, blocking collectives: 44.2 us -> none  [body(): lax.psum((edge_in_grad, edge_mid_grad, edge_bias_grad, node_in_grad, node...]
    another operation x12 -> x0, local copies, waits for them, and re-layouts: 30.2 us -> none  [the longest x1 11.6 us: matmul(): flat = values.reshape(-1, values.shape[-1])]
    ppermute x12 -> x0, starting transfers between devices: 27.8 us -> none  [shifted(): return lax.ppermute(block, axis, route)]
    ppermute x12 -> x0, waiting for transfers between devices: 26.7 us -> none  [shifted(): return lax.ppermute(block, axis, route)]
  transfers between devices with their start and end apart: 13 -> 1, of which waited for: 9 -> 1; matrix products, arithmetic and copies ran while one was open for 24% -> 0% of each run, Pallas kernels for 0% -> 0%
where the time goes in v1:
time: 252 us; the launch traced here: 251 us
  waiting for transfers between devices  128 us (51%)
  Pallas kernels  94.4 us (37%)
  between operations  14.1 us (6%)
  local copies, waits for them, and re-layouts  13.4 us (5%)
    psum x1, waiting for transfers between devices, body(): edge_total = lax.psum(edge_total, 'dom')  128 us
    pallas_call x3, Pallas kernels, on_elements(): pl.pallas_call(kernel, grid_spec=pltpu.PrefetchScalarGridSpec(num_scalar_...  58.3 us
    pallas_call x2, Pallas kernels, make_consistent(): pl.pallas_call(functools.partial(exchange_kernel, devices), out_shape=jax...  36.1 us
    unnamed x34, local copies, waits for them, and re-layouts  10.1 us
  transfers between devices with their start and end apart: 1, of which 1 were waited for; matrix products, arithmetic and copies ran while one was open for 0% of the time, Pallas kernels for 0%

profile of v1, /device:TPU:0, one launch (start us, length us, event | category | flops | bytes accessed | tf_op | source)
XLA Modules:
  0.0 250.8 jit_solution(9083917414095878114)
XLA Ops:
  7.2 0.0 all-reduce.3.cloned.1.call-start
  7.2 0.7 reshape.27.order
  8.0 0.9 copy-done.4
  8.9 0.9 copy-done.6
  9.8 0.7 copy-done.9
  10.4 0.7 copy-done.11
  11.1 13.4 %shard_map.161 = (f32[4096,128]{1,0:T(8,128)S(1)}, f32[4096,128]{1,0:T(8,128)S(1)}, f32[4096,128]{1,0:T(8,128)}) custom-call(s32[1,8]{1,0:T(1,128)S(1)} %copy-done.11, f32[4096,128]{1,0:T(8,128)} %feat.1, s32[8,1,512]{2,1,0:T(1,128)S(1)} %reshape.27.order, f32[256,128]{1,0:T(8,128)S(1)} %copy-done.4, f32[2,128,128]{2,1,0:T(8,128)S(1)} %copy-done.6, ...), custom_call_target="tpu_custom_call" | custom-call | flops 2952790016 | bytes 8388608 | tf_op jit(solution)/shard_map/pallas_call | solution.py:297
  24.5 1.3 copy-done.13
  25.8 1.3 copy-done.15
  27.2 1.6 copy-done.1
  28.8 18.1 %shard_map.162.gathered_ref = f32[4096,128]{1,0:T(8,128)S(1)} custom-call(f32[4096,128]{1,0:T(8,128)S(1)} %copy-done.1), custom_call_target="tpu_custom_call" | custom-call | tf_op jit(solution)/shard_map/pallas_call | solution.py:404
  46.9 0.0 copy-start
  46.9 1.3 copy-done
  48.2 16.3 %shard_map.163 = (f32[4096,128]{1,0:T(8,128)}, f32[4096,128]{1,0:T(8,128)S(1)}, f32[4096,128]{1,0:T(8,128)S(1)}, f32[520,128]{1,0:T(8,128)}) custom-call(s32[1,8]{1,0:T(1,128)S(1)} %copy-done.12, f32[4096,128]{1,0:T(8,128)} %copy-done.13, f32[4096,128]{1,0:T(8,128)} %copy-done, f32[4096,128]{1,0:T(8,128)} %cotangent.1, s32[8,1,512]{2,1,0:T(1,128)S(1)} %reshape.27.order, ...), custom_call_target="tpu_custom_call" | custom-call | flops 6442450944 | bytes 8388608 | tf_op jit(solution)/shard_map/pallas_call | solution.py:297
  64.6 1.3 copy-done.16
  65.9 18.0 %shard_map.164.around_ref = f32[4096,128]{1,0:T(8,128)S(1)} custom-call(f32[4096,128]{1,0:T(8,128)S(1)} %get-tuple-element.20.field_in), custom_call_target="tpu_custom_call" | custom-call | tf_op jit(solution)/shard_map/pallas_call | solution.py:404
  84.0 28.6 %shard_map.165 = (f32[4096,128]{1,0:T(8,128)}, f32[520,128]{1,0:T(8,128)}) custom-call(s32[1,8]{1,0:T(1,128)S(1)} %copy-done.12, f32[4096,128]{1,0:T(8,128)S(1)} %copy-done.14, f32[4096,128]{1,0:T(8,128)S(1)} %shard_map.164.around_ref, f32[4096,128]{1,0:T(8,128)} %copy-done.15, f32[4096,128]{1,0:T(8,128)} %copy-done.16, s32[8,1,512]{2,1,0:T(1,128)S(1)} %reshape.27.order, ...), custom_call_target="tpu_custom_call" | custom-call | flops 8858370048 | bytes 8388608 | tf_op jit(solution)/shard_map/pallas_call | solution.py:297
  112.5 0.0 all-reduce.3.cloned.1.call-update
  112.5 127.8 %all-reduce.3.cloned.1.call-done = (f32[520,128]{1,0:T(8,128)}, f32[520,128]{1,0:T(8,128)}) async-done(((f32[520,128]{1,0:T(8,128)}, f32[520,128]{1,0:T(8,128)}), (f32[520,128]{1,0:T(8,128)}, f32[520,128]{1,0:T(8,128)})) %all-reduce.3.cloned.1.call-update) | async-done | bytes 532496 | tf_op jit(solution)/shard_map/psum | solution.py:470
  240.3 1.1 broadcast_multiply_fusion
  241.4 0.6 slice.29
  242.0 0.7 fusion
  242.7 0.6 slice.26
  243.3 0.7 fusion.1
  (24 shorter events, 0.0 us)
Async XLA Ops:
  7.2 233.1 %all-reduce.3.cloned.1.call-start = ((), (), s32[]{:S(2)}) async-start(), calls=%async_computation | async-start | bytes 1064960 | tf_op jit(solution)/shard_map/psum | solution.py:470
  7.9 0.9 copy-start.4
  8.9 0.9 copy-start.6
  9.8 0.7 copy-start.9
  10.4 0.7 copy-start.11
  24.5 1.3 copy-start.13
  25.8 1.3 copy-start.15
  27.2 1.6 copy-start.1
  28.8 19.5 %copy-start.2 = (f32[256,128]{1,0:T(8,128)S(1)}, f32[256,128]{1,0:T(8,128)}, u32[]{:S(2)}) copy-start(f32[256,128]{1,0:T(8,128)} %w_in.4) | copy-start | bytes 393220
  28.8 19.5 %copy-start.3 = (f32[2,128,128]{2,1,0:T(8,128)S(1)}, f32[2,128,128]{2,1,0:T(8,128)}, u32[]{:S(2)}) copy-start(f32[2,128,128]{2,1,0:T(8,128)} %w_mid.4) | copy-start | bytes 393220
  28.8 19.5 %copy-start.8 = (f32[3,128]{1,0:T(4,128)S(1)}, f32[3,128]{1,0:T(4,128)}, u32[]{:S(2)}) copy-start(f32[3,128]{1,0:T(4,128)} %bias.4) | copy-start | bytes 4612
  28.8 19.5 %copy-start.12 = (s32[1,8]{1,0:T(1,128)S(1)}, s32[1,8]{1,0:T(1,128)}, u32[]{:S(2)}) copy-start(s32[1,8]{1,0:T(1,128)} %place.5) | copy-start | bytes 100
  46.9 1.3 copy-start
  64.6 1.3 copy-start.16
  65.9 18.0 %copy-start.5 = (f32[256,128]{1,0:T(8,128)S(1)}, f32[256,128]{1,0:T(8,128)}, u32[]{:S(2)}) copy-start(f32[256,128]{1,0:T(8,128)} %w_in.5) | copy-start | bytes 393220
  65.9 18.0 %copy-start.7 = (f32[2,128,128]{2,1,0:T(8,128)S(1)}, f32[2,128,128]{2,1,0:T(8,128)}, u32[]{:S(2)}) copy-start(f32[2,128,128]{2,1,0:T(8,128)} %w_mid.5) | copy-start | bytes 393220
  65.9 18.0 %copy-start.10 = (f32[3,128]{1,0:T(4,128)S(1)}, f32[3,128]{1,0:T(4,128)}, u32[]{:S(2)}) copy-start(f32[3,128]{1,0:T(4,128)} %bias.5) | copy-start | bytes 4612
  65.9 18.0 %copy-start.14 = (f32[4096,128]{1,0:T(8,128)S(1)}, f32[4096,128]{1,0:T(8,128)}, u32[]{:S(2)}) copy-start(f32[4096,128]{1,0:T(8,128)} %copy-done.13) | copy-start | bytes 6291460
Sparse Core Ops, SparseCore 0:
  112.7 127.5 all-reduce.2

commit v2 on v1

--- a/solution.py
+++ b/solution.py
@@ -418,11 +418,87 @@
     )(field)
 
 
-def unpack(total, scale):
-    channels = total.shape[1]
-    c = channels
-    total = total * scale
-    return total[:2 * c], total[2 * c:4 * c].reshape(2, c, c), total[4 * c:4 * c + 3]
+def total_kernel(devices, scale, edge, node, *refs):
+    outs, (work, result, arriving, send_sem, recv_sem) = refs[:6], refs[6:]
+    me = lax.axis_index("dom")
+    bits = devices.bit_length() - 1
+    side = [me // 2**k % 2 for k in range(bits)]
+    partner = [me + 2**k - 2 * 2**k * side[k] for k in range(bits)]
+    barrier = pltpu.get_barrier_semaphore()
+    for k in range(bits):
+        pl.semaphore_signal(barrier, inc=1, device_id=(partner[k],), device_id_type=pl.DeviceIdType.MESH)
+    each = edge.shape[0]
+    rows = work.shape[0]
+    work[0:each] = edge[...]
+    work[each:2 * each] = node[...]
+    if rows > 2 * each:
+        work[2 * each:rows] = jnp.zeros((rows - 2 * each, work.shape[1]), F32)
+    pl.semaphore_wait(barrier, bits)
+
+    def send(source, target, step, to):
+        return pltpu.make_async_remote_copy(
+            src_ref=source,
+            dst_ref=target,
+            send_sem=send_sem.at[step],
+            recv_sem=recv_sem.at[step],
+            device_id=(to,),
+            device_id_type=pl.DeviceIdType.MESH,
+        )
+
+    start = jnp.int32(0)
+    offset = 0
+    size = rows
+    starts = []
+    for k in range(bits):
+        size //= 2
+        keep = pl.multiple_of(start + side[k] * size, SIDE)
+        give = pl.multiple_of(start + (1 - side[k]) * size, SIDE)
+        landing = arriving.at[pl.ds(offset, size)]
+        copy = send(work.at[pl.ds(give, size)], landing, k, partner[k])
+        copy.start()
+        copy.wait()
+        work[pl.ds(keep, size)] += arriving[offset:offset + size]
+        offset += size
+        start = keep
+        starts.append(keep)
+    result[pl.ds(start, size)] = work[pl.ds(start, size)] * scale
+    for k in reversed(range(bits)):
+        block = result.at[pl.ds(starts[k], size)]
+        copy = send(block, block, bits + k, partner[k])
+        copy.start()
+        copy.wait()
+        size *= 2
+    for base, (first, middle, bias) in ((0, outs[:3]), (each, outs[3:])):
+        c = result.shape[1]
+        first[...] = result[base:base + 2 * c]
+        middle[...] = result[base + 2 * c:base + 4 * c]
+        bias[...] = result[base + 4 * c:base + 4 * c + 3]
+
+
+def sum_over_devices(edge, node, scale, collective):
+    devices = lax.axis_size("dom")
+    channels = edge.shape[1]
+    unit = SIDE * devices
+    rows = -(-2 * edge.shape[0] // unit) * unit
+    group = [jax.ShapeDtypeStruct((n, channels), F32) for n in (2 * channels, 2 * channels, 3)]
+    steps = 2 * (devices.bit_length() - 1)
+    in_vmem = pl.BlockSpec(memory_space=pltpu.VMEM)
+    outs = pl.pallas_call(
+        functools.partial(total_kernel, devices, scale),
+        out_shape=group + group,
+        in_specs=[in_vmem] * 2,
+        out_specs=[in_vmem] * 6,
+        scratch_shapes=[pltpu.VMEM((rows, channels), F32)] * 3
+        + [pltpu.SemaphoreType.DMA((steps,))] * 2,
+        compiler_params=pltpu.CompilerParams(
+            collective_id=collective, has_side_effects=True, vmem_limit_bytes=VMEM_BYTES
+        ),
+    )(edge, node)
+    middle = (2, channels, channels)
+    return (
+        outs[0], outs[1].reshape(middle), outs[2],
+        outs[3], outs[4].reshape(middle), outs[5],
+    )
 
 
 def body(
@@ -461,15 +537,13 @@
         3, [True, False, False], True, [wide] * 8, cost(12 * NODES_EL),
     )
     around = make_consistent(around, 1)
-    node_total = lax.psum(node_total, "dom")
     tall = pltpu.VMEM((pairs, 2 * channels), BF16)
     feat_grad, edge_total = on_elements(
         edge_backward_kernel, element_place, [lattice, around, summed, direct], [False] * 4, edge, lattice_of,
         1, [True], True, [cube] * 5 + [tall] * 2 + [wide] * 7, cost(3 * pairs),
     )
-    edge_total = lax.psum(edge_total, "dom")
     scale = 1.0 / math.sqrt(lax.axis_size("dom") * ELEM_DEV * NODES_EL)
-    return (new_feat, feat_grad) + unpack(edge_total, scale) + unpack(node_total, scale)
+    return (new_feat, feat_grad) + sum_over_devices(edge_total, node_total, scale, 2)
 
 
 def solution(mesh):

time: 252 us -> 145 us (0.58)
  waiting for transfers between devices: 128 us -> 0 us
  Pallas kernels: 94.4 us -> 129 us
  between operations: 14.1 us -> 0.73 us
    psum x1 -> x0, waiting for transfers between devices: 128 us -> none  [body(): edge_total = lax.psum(edge_total, 'dom')]
    pallas_call x0 -> x1, Pallas kernels: none -> 35.3 us  [sum_over_devices(): pl.pallas_call(functools.partial(total_kernel, devices, scale), out_shape...]
    unnamed x34 -> x40, local copies, waits for them, and re-layouts: 10.1 us -> 13.8 us
    slice x4 -> x0, local copies, waits for them, and re-layouts: 2.59 us -> none  [the longest x2 1.43 us: unpack(): total[2 * c:4 * c].reshape(2, c, c)]
  transfers between devices with their start and end apart: 1 -> 0, of which waited for: 1 -> 0; matrix products, arithmetic and copies ran while one was open for 0% -> 0% of each run, Pallas kernels for 0% -> 0%
where the time goes in v2:
time: 145 us; the launch traced here: 144 us
  Pallas kernels  129 us (89%)
  local copies, waits for them, and re-layouts  14.6 us (10%)
    pallas_call x3, Pallas kernels, on_elements(): pl.pallas_call(kernel, grid_spec=pltpu.PrefetchScalarGridSpec(num_scalar_...  57.7 us
    pallas_call x2, Pallas kernels, make_consistent(): pl.pallas_call(functools.partial(exchange_kernel, devices), out_shape=jax...  36.1 us
    pallas_call x1, Pallas kernels, sum_over_devices(): pl.pallas_call(functools.partial(total_kernel, devices, scale), out_shape...  35.3 us
    unnamed x40, local copies, waits for them, and re-layouts  13.8 us

profile of v2, /device:TPU:0, one launch (start us, length us, event | category | flops | bytes accessed | tf_op | source)
XLA Modules:
  0.0 144.3 jit_solution(17715699610226675727)
XLA Ops:
  0.6 0.7 reshape.27.order
  1.4 0.0 copy-start.4
  1.4 0.9 copy-done.4
  2.3 0.9 copy-done.6
  3.2 0.7 copy-done.9
  3.9 0.7 copy-done.11
  4.5 13.4 %shard_map.161 = (f32[4096,128]{1,0:T(8,128)S(1)}, f32[4096,128]{1,0:T(8,128)S(1)}, f32[4096,128]{1,0:T(8,128)}) custom-call(s32[1,8]{1,0:T(1,128)S(1)} %copy-done.11, f32[4096,128]{1,0:T(8,128)} %feat.1, s32[8,1,512]{2,1,0:T(1,128)S(1)} %reshape.27.order, f32[256,128]{1,0:T(8,128)S(1)} %copy-done.4, f32[2,128,128]{2,1,0:T(8,128)S(1)} %copy-done.6, ...), custom_call_target="tpu_custom_call" | custom-call | flops 2952790016 | bytes 8388608 | tf_op jit(solution)/shard_map/pallas_call | solution.py:297
  18.0 1.3 copy-done.13
  19.3 1.3 copy-done.15
  20.6 1.6 %copy-done.1 = f32[4096,128]{1,0:T(8,128)S(1)} copy-done((f32[4096,128]{1,0:T(8,128)S(1)}, f32[4096,128]{1,0:T(8,128)}, u32[]{:S(2)}) %copy-start.1) | copy-done | bytes 2097176
  22.2 18.1 %shard_map.162.gathered_ref = f32[4096,128]{1,0:T(8,128)S(1)} custom-call(f32[4096,128]{1,0:T(8,128)S(1)} %copy-done.1), custom_call_target="tpu_custom_call" | custom-call | tf_op jit(solution)/shard_map/pallas_call | solution.py:404
  40.3 0.0 copy-start
  40.4 1.3 copy-done
  41.7 16.0 %shard_map.163 = (f32[4096,128]{1,0:T(8,128)}, f32[4096,128]{1,0:T(8,128)S(1)}, f32[4096,128]{1,0:T(8,128)S(1)}, f32[520,128]{1,0:T(8,128)S(1)}) custom-call(s32[1,8]{1,0:T(1,128)S(1)} %copy-done.12, f32[4096,128]{1,0:T(8,128)} %copy-done.13, f32[4096,128]{1,0:T(8,128)} %copy-done, f32[4096,128]{1,0:T(8,128)} %cotangent.1, s32[8,1,512]{2,1,0:T(1,128)S(1)} %reshape.27.order, ...), custom_call_target="tpu_custom_call" | custom-call | flops 6442450944 | bytes 8388608 | tf_op jit(solution)/shard_map/pallas_call | solution.py:297
  57.7 1.4 copy-done.16
  59.1 18.0 %shard_map.164.around_ref = f32[4096,128]{1,0:T(8,128)S(1)} custom-call(f32[4096,128]{1,0:T(8,128)S(1)} %get-tuple-element.26.field_in), custom_call_target="tpu_custom_call" | custom-call | tf_op jit(solution)/shard_map/pallas_call | solution.py:404
  77.1 28.2 %shard_map.165 = (f32[4096,128]{1,0:T(8,128)}, f32[520,128]{1,0:T(8,128)S(1)}) custom-call(s32[1,8]{1,0:T(1,128)S(1)} %copy-done.12, f32[4096,128]{1,0:T(8,128)S(1)} %copy-done.14, f32[4096,128]{1,0:T(8,128)S(1)} %shard_map.164.around_ref, f32[4096,128]{1,0:T(8,128)} %copy-done.15, f32[4096,128]{1,0:T(8,128)} %copy-done.16, s32[8,1,512]{2,1,0:T(1,128)S(1)} %reshape.27.order, ...), custom_call_target="tpu_custom_call" | custom-call | flops 8858370048 | bytes 8388608 | tf_op jit(solution)/shard_map/pallas_call | solution.py:297
  105.3 35.3 %shard_map.166 = (f32[256,128]{1,0:T(8,128)S(1)}, f32[256,128]{1,0:T(8,128)S(1)}, f32[3,128]{1,0:T(4,128)S(1)}, f32[256,128]{1,0:T(8,128)S(1)}, f32[256,128]{1,0:T(8,128)S(1)}, /*index=5*/f32[3,128]{1,0:T(4,128)S(1)}) custom-call(f32[520,128]{1,0:T(8,128)S(1)} %get-tuple-element.30.edge, f32[520,128]{1,0:T(8,128)S(1)} %get-tuple-element.31.node), custom_call_target="tpu_custom_call" | custom-call | tf_op jit(solution)/shard_map/pallas_call | solution.py:486
  140.6 0.7 copy.24
  141.2 0.7 copy.25
  141.9 0.6 copy.26
  142.5 0.7 copy.27
  143.1 0.7 copy.28
  143.8 0.6 copy.29
  (23 shorter events, 0.0 us)
Async XLA Ops:
  1.4 0.9 copy-start.4
  2.3 0.9 copy-start.6
  3.2 0.7 copy-start.9
  3.9 0.7 copy-start.11
  18.0 1.3 copy-start.13
  19.3 1.3 copy-start.15
  20.6 1.6 %copy-start.1 = (f32[4096,128]{1,0:T(8,128)S(1)}, f32[4096,128]{1,0:T(8,128)}, u32[]{:S(2)}) copy-start(f32[4096,128]{1,0:T(8,128)} %get-tuple-element.24.field_in) | copy-start | bytes 6291460
  22.2 19.5 %copy-start.2 = (f32[256,128]{1,0:T(8,128)S(1)}, f32[256,128]{1,0:T(8,128)}, u32[]{:S(2)}) copy-start(f32[256,128]{1,0:T(8,128)} %w_in.4) | copy-start | bytes 393220
  22.2 19.5 %copy-start.3 = (f32[2,128,128]{2,1,0:T(8,128)S(1)}, f32[2,128,128]{2,1,0:T(8,128)}, u32[]{:S(2)}) copy-start(f32[2,128,128]{2,1,0:T(8,128)} %w_mid.4) | copy-start | bytes 393220
  22.2 19.5 %copy-start.8 = (f32[3,128]{1,0:T(4,128)S(1)}, f32[3,128]{1,0:T(4,128)}, u32[]{:S(2)}) copy-start(f32[3,128]{1,0:T(4,128)} %bias.4) | copy-start | bytes 4612
  22.2 19.5 %copy-start.12 = (s32[1,8]{1,0:T(1,128)S(1)}, s32[1,8]{1,0:T(1,128)}, u32[]{:S(2)}) copy-start(s32[1,8]{1,0:T(1,128)} %place.5) | copy-start | bytes 100
  40.3 1.3 copy-start
  57.7 1.4 copy-start.16
  59.1 18.0 %copy-start.5 = (f32[256,128]{1,0:T(8,128)S(1)}, f32[256,128]{1,0:T(8,128)}, u32[]{:S(2)}) copy-start(f32[256,128]{1,0:T(8,128)} %w_in.5) | copy-start | bytes 393220
  59.1 18.0 %copy-start.7 = (f32[2,128,128]{2,1,0:T(8,128)S(1)}, f32[2,128,128]{2,1,0:T(8,128)}, u32[]{:S(2)}) copy-start(f32[2,128,128]{2,1,0:T(8,128)} %w_mid.5) | copy-start | bytes 393220
  59.1 18.0 %copy-start.10 = (f32[3,128]{1,0:T(4,128)S(1)}, f32[3,128]{1,0:T(4,128)}, u32[]{:S(2)}) copy-start(f32[3,128]{1,0:T(4,128)} %bias.5) | copy-start | bytes 4612
  59.1 18.0 %copy-start.14 = (f32[4096,128]{1,0:T(8,128)S(1)}, f32[4096,128]{1,0:T(8,128)}, u32[]{:S(2)}) copy-start(f32[4096,128]{1,0:T(8,128)} %copy-done.13) | copy-start | bytes 6291460

commit v3 on v2

--- a/solution.py
+++ b/solution.py
@@ -16,7 +16,7 @@
 
 F32 = jnp.float32
 BF16 = jnp.bfloat16
-VMEM_BYTES = 48 * 2**20
+VMEM_BYTES = 20 * 2**20
 PAIRS = ((2, True), (2, False), (0, True), (0, False), (1, True), (1, False))
 
 
@@ -418,22 +418,35 @@
     )(field)
 
 
+def digits(devices):
+    found = []
+    low = 1
+    while low < devices:
+        radix = 2 if low == 1 or devices // low % 4 else 4
+        found.append((low, radix))
+        low *= radix
+    return found
+
+
 def total_kernel(devices, scale, edge, node, *refs):
     outs, (work, result, arriving, send_sem, recv_sem) = refs[:6], refs[6:]
     me = lax.axis_index("dom")
-    bits = devices.bit_length() - 1
-    side = [me // 2**k % 2 for k in range(bits)]
-    partner = [me + 2**k - 2 * 2**k * side[k] for k in range(bits)]
+    stages = digits(devices)
+    peers = [
+        [(me // low % radix + j) % radix for j in range(radix)] for low, radix in stages
+    ]
     barrier = pltpu.get_barrier_semaphore()
-    for k in range(bits):
-        pl.semaphore_signal(barrier, inc=1, device_id=(partner[k],), device_id_type=pl.DeviceIdType.MESH)
+    for (low, radix), digit in zip(stages, peers):
+        for j in range(1, radix):
+            to = me + (digit[j] - digit[0]) * low
+            pl.semaphore_signal(barrier, inc=1, device_id=(to,), device_id_type=pl.DeviceIdType.MESH)
     each = edge.shape[0]
     rows = work.shape[0]
     work[0:each] = edge[...]
     work[each:2 * each] = node[...]
     if rows > 2 * each:
         work[2 * each:rows] = jnp.zeros((rows - 2 * each, work.shape[1]), F32)
-    pl.semaphore_wait(barrier, bits)
+    pl.semaphore_wait(barrier, sum(radix - 1 for _, radix in stages))
 
     def send(source, target, step, to):
         return pltpu.make_async_remote_copy(
@@ -448,26 +461,40 @@
     start = jnp.int32(0)
     offset = 0
     size = rows
+    step = 0
     starts = []
-    for k in range(bits):
-        size //= 2
-        keep = pl.multiple_of(start + side[k] * size, SIDE)
-        give = pl.multiple_of(start + (1 - side[k]) * size, SIDE)
-        landing = arriving.at[pl.ds(offset, size)]
-        copy = send(work.at[pl.ds(give, size)], landing, k, partner[k])
-        copy.start()
-        copy.wait()
-        work[pl.ds(keep, size)] += arriving[offset:offset + size]
-        offset += size
-        start = keep
-        starts.append(keep)
+    for (low, radix), digit in zip(stages, peers):
+        size //= radix
+        copies = []
+        landings = []
+        for j in range(1, radix):
+            give = pl.multiple_of(start + digit[j] * size, SIDE)
+            to = me + (digit[j] - digit[0]) * low
+            copy = send(work.at[pl.ds(give, size)], arriving.at[pl.ds(offset, size)], step, to)
+            copy.start()
+            copies.append(copy)
+            landings.append(offset)
+            offset += size
+            step += 1
+        starts.append(start)
+        start = pl.multiple_of(start + digit[0] * size, SIDE)
+        for copy, landing in zip(copies, landings):
+            copy.wait()
+            work[pl.ds(start, size)] += arriving[landing:landing + size]
     result[pl.ds(start, size)] = work[pl.ds(start, size)] * scale
-    for k in reversed(range(bits)):
-        block = result.at[pl.ds(starts[k], size)]
-        copy = send(block, block, bits + k, partner[k])
-        copy.start()
-        copy.wait()
-        size *= 2
+    for (low, radix), digit, before in reversed(list(zip(stages, peers, starts))):
+        block = result.at[pl.ds(start, size)]
+        copies = []
+        for j in range(1, radix):
+            to = me + (digit[j] - digit[0]) * low
+            copy = send(block, block, step, to)
+            copy.start()
+            copies.append(copy)
+            step += 1
+        for copy in copies:
+            copy.wait()
+        start = before if isinstance(before, int) else pl.multiple_of(before, SIDE)
+        size *= radix
     for base, (first, middle, bias) in ((0, outs[:3]), (each, outs[3:])):
         c = result.shape[1]
         first[...] = result[base:base + 2 * c]
@@ -481,7 +508,7 @@
     unit = SIDE * devices
     rows = -(-2 * edge.shape[0] // unit) * unit
     group = [jax.ShapeDtypeStruct((n, channels), F32) for n in (2 * channels, 2 * channels, 3)]
-    steps = 2 * (devices.bit_length() - 1)
+    steps = 2 * sum(radix - 1 for _, radix in digits(devices))
     in_vmem = pl.BlockSpec(memory_space=pltpu.VMEM)
     outs = pl.pallas_call(
         functools.partial(total_kernel, devices, scale),

time: 145 us -> 125 us (0.86)
  Pallas kernels: 129 us -> 115 us
  local copies, waits for them, and re-layouts: 14.6 us -> 9.27 us
    pallas_call x1, Pallas kernels: 35.3 us -> 24.9 us  [sum_over_devices(): pl.pallas_call(functools.partial(total_kernel, devices, scale), out_shape...]
    unnamed x40 -> x30, local copies, waits for them, and re-layouts: 13.8 us -> 8.54 us
    pallas_call x3, Pallas kernels: 57.7 us -> 53.7 us  [on_elements(): pl.pallas_call(kernel, grid_spec=pltpu.PrefetchScalarGridSpec(num_scalar_...]
where the time goes in v3:
time: 125 us
  Pallas kernels  115 us (92%)
  local copies, waits for them, and re-layouts  9.27 us (7%)
    pallas_call x3, Pallas kernels, on_elements(): pl.pallas_call(kernel, grid_spec=pltpu.PrefetchScalarGridSpec(num_scalar_...  53.7 us
    pallas_call x2, Pallas kernels, make_consistent(): pl.pallas_call(functools.partial(exchange_kernel, devices), out_shape=jax...  36.1 us
    pallas_call x1, Pallas kernels, sum_over_devices(): pl.pallas_call(functools.partial(total_kernel, devices, scale), out_shape...  24.9 us
    unnamed x30, local copies, waits for them, and re-layouts  8.54 us

profile of v3, /device:TPU:0, one launch (start us, length us, event | category | flops | bytes accessed | tf_op | source)
XLA Modules:
  0.0 124.8 jit_solution(3279015232341712017)
XLA Ops:
  0.6 0.7 reshape.27.order
  1.4 0.0 copy-start
  1.4 1.6 %copy-done = f32[4096,128]{1,0:T(8,128)S(1)} copy-done((f32[4096,128]{1,0:T(8,128)S(1)}, f32[4096,128]{1,0:T(8,128)}, u32[]{:S(2)}) %copy-start) | copy-done | bytes 2097176
  3.0 0.9 copy-done.4
  3.9 0.9 copy-done.6
  4.8 0.7 copy-done.9
  5.5 0.7 copy-done.11
  6.1 11.5 %shard_map.161 = (f32[4096,128]{1,0:T(8,128)S(1)}, f32[4096,128]{1,0:T(8,128)S(1)}, f32[4096,128]{1,0:T(8,128)S(1)}) custom-call(s32[1,8]{1,0:T(1,128)S(1)} %copy-done.11, f32[4096,128]{1,0:T(8,128)S(1)} %copy-done, s32[8,1,512]{2,1,0:T(1,128)S(1)} %reshape.27.order, f32[256,128]{1,0:T(8,128)S(1)} %copy-done.4, f32[2,128,128]{2,1,0:T(8,128)S(1)} %copy-done.6, ...), custom_call_target="tpu_custom_call" | custom-call | flops 2952790016 | bytes 8388608 | tf_op jit(solution)/shard_map/pallas_call | solution.py:297
  17.7 0.0 copy-start.1
  17.7 0.0 copy-start.2
  17.7 0.0 copy-start.3
  17.7 0.0 copy-start.8
  17.7 18.1 %shard_map.162.gathered_ref = f32[4096,128]{1,0:T(8,128)S(1)} custom-call(f32[4096,128]{1,0:T(8,128)S(1)} %get-tuple-element.24.field_in), custom_call_target="tpu_custom_call" | custom-call | tf_op jit(solution)/shard_map/pallas_call | solution.py:404
  35.9 0.0 copy-done.1
  35.9 14.9 %shard_map.163 = (f32[4096,128]{1,0:T(8,128)}, f32[4096,128]{1,0:T(8,128)S(1)}, f32[4096,128]{1,0:T(8,128)S(1)}, f32[520,128]{1,0:T(8,128)S(1)}) custom-call(s32[1,8]{1,0:T(1,128)S(1)} %copy-done.11, f32[4096,128]{1,0:T(8,128)S(1)} %get-tuple-element.23.lattice_ref, f32[4096,128]{1,0:T(8,128)S(1)} %shard_map.162.gathered_ref, f32[4096,128]{1,0:T(8,128)S(1)} %copy-done.1, ...), custom_call_target="tpu_custom_call" | custom-call | flops 6442450944 | bytes 8388608 | tf_op jit(solution)/shard_map/pallas_call | solution.py:297
  50.8 17.9 %shard_map.164.around_ref = f32[4096,128]{1,0:T(8,128)S(1)} custom-call(f32[4096,128]{1,0:T(8,128)S(1)} %get-tuple-element.26.field_in), custom_call_target="tpu_custom_call" | custom-call | tf_op jit(solution)/shard_map/pallas_call | solution.py:404
  68.8 27.3 %shard_map.165 = (f32[4096,128]{1,0:T(8,128)}, f32[520,128]{1,0:T(8,128)S(1)}) custom-call(s32[1,8]{1,0:T(1,128)S(1)} %copy-done.11, f32[4096,128]{1,0:T(8,128)S(1)} %get-tuple-element.23.lattice_ref, f32[4096,128]{1,0:T(8,128)S(1)} %shard_map.164.around_ref, f32[4096,128]{1,0:T(8,128)S(1)} %get-tuple-element.27.summed_ref, ...), custom_call_target="tpu_custom_call" | custom-call | flops 8858370048 | bytes 8388608 | tf_op jit(solution)/shard_map/pallas_call | solution.py:297
  96.1 24.9 %shard_map.166 = (f32[256,128]{1,0:T(8,128)S(1)}, f32[256,128]{1,0:T(8,128)S(1)}, f32[3,128]{1,0:T(4,128)S(1)}, f32[256,128]{1,0:T(8,128)S(1)}, f32[256,128]{1,0:T(8,128)S(1)}, /*index=5*/f32[3,128]{1,0:T(4,128)S(1)}) custom-call(f32[520,128]{1,0:T(8,128)S(1)} %get-tuple-element.30.edge, f32[520,128]{1,0:T(8,128)S(1)} %get-tuple-element.31.node), custom_call_target="tpu_custom_call" | custom-call | tf_op jit(solution)/shard_map/pallas_call | solution.py:513
  121.0 0.7 copy.24
  121.7 0.7 copy.25
  122.3 0.6 copy.26
  122.9 0.7 copy.27
  123.6 0.7 copy.28
  124.2 0.6 copy.29
  (13 shorter events, 0.0 us)
Async XLA Ops:
  1.4 1.6 %copy-start = (f32[4096,128]{1,0:T(8,128)S(1)}, f32[4096,128]{1,0:T(8,128)}, u32[]{:S(2)}) copy-start(f32[4096,128]{1,0:T(8,128)} %feat.1) | copy-start | bytes 6291460
  3.0 0.9 copy-start.4
  3.9 0.9 copy-start.6
  4.8 0.7 copy-start.9
  5.5 0.7 copy-start.11
  17.7 18.2 %copy-start.1 = (f32[4096,128]{1,0:T(8,128)S(1)}, f32[4096,128]{1,0:T(8,128)}, u32[]{:S(2)}) copy-start(f32[4096,128]{1,0:T(8,128)} %cotangent.1) | copy-start | bytes 6291460
  17.7 18.2 %copy-start.2 = (f32[256,128]{1,0:T(8,128)S(1)}, f32[256,128]{1,0:T(8,128)}, u32[]{:S(2)}) copy-start(f32[256,128]{1,0:T(8,128)} %w_in.4) | copy-start | bytes 393220
  17.7 18.2 %copy-start.3 = (f32[2,128,128]{2,1,0:T(8,128)S(1)}, f32[2,128,128]{2,1,0:T(8,128)}, u32[]{:S(2)}) copy-start(f32[2,128,128]{2,1,0:T(8,128)} %w_mid.4) | copy-start | bytes 393220
  17.7 18.2 %copy-start.8 = (f32[3,128]{1,0:T(4,128)S(1)}, f32[3,128]{1,0:T(4,128)}, u32[]{:S(2)}) copy-start(f32[3,128]{1,0:T(4,128)} %bias.4) | copy-start | bytes 4612
  50.8 18.0 %copy-start.5 = (f32[256,128]{1,0:T(8,128)S(1)}, f32[256,128]{1,0:T(8,128)}, u32[]{:S(2)}) copy-start(f32[256,128]{1,0:T(8,128)} %w_in.5) | copy-start | bytes 393220
  50.8 18.0 %copy-start.7 = (f32[2,128,128]{2,1,0:T(8,128)S(1)}, f32[2,128,128]{2,1,0:T(8,128)}, u32[]{:S(2)}) copy-start(f32[2,128,128]{2,1,0:T(8,128)} %w_mid.5) | copy-start | bytes 393220
  50.8 18.0 %copy-start.10 = (f32[3,128]{1,0:T(4,128)S(1)}, f32[3,128]{1,0:T(4,128)}, u32[]{:S(2)}) copy-start(f32[3,128]{1,0:T(4,128)} %bias.5) | copy-start | bytes 4612

commit v4 on v3

--- a/solution.py
+++ b/solution.py
@@ -353,22 +353,25 @@
         for side in range(2):
             peers = peers + jnp.where(exists[axis][side], jnp.int32(1), jnp.int32(0))
     pl.semaphore_wait(barrier, peers)
-    for axis in (2, 1, 0):
+    def part(axis, side, half):
         weight = (4, 2, 1)[axis]
-        sides = [[p for p in range(ELEM_DEV) if p // weight % 2 == side] for side in range(2)]
+        return [p for p in range(ELEM_DEV) if p // weight % 2 == side and (axis == 0 or p // 4 == half)]
+
+    def begin(axis, half):
         copies = []
         for side in range(2):
-            at = 0
-            for element in sides[side]:
+            first = at = half * outgoing.shape[2] // 2
+            for element in part(axis, side, half):
                 for rows, count in plane(axis, element, side):
                     outgoing[axis, side, at:at + count] = field[rows]
                     at += count
+            span = pl.ds(first, at - first)
             copies.append(
                 pltpu.make_async_remote_copy(
-                    src_ref=outgoing.at[axis, side],
-                    dst_ref=arriving.at[axis, 1 - side],
-                    send_sem=send_sem.at[axis, side],
-                    recv_sem=recv_sem.at[axis, 1 - side],
+                    src_ref=outgoing.at[axis, side, span],
+                    dst_ref=arriving.at[axis, 1 - side, span],
+                    send_sem=send_sem.at[axis, side, half],
+                    recv_sem=recv_sem.at[axis, 1 - side, half],
                     device_id=(partner[axis][side],),
                     device_id_type=pl.DeviceIdType.MESH,
                 )
@@ -379,22 +382,34 @@
             def _():
                 copies[side].start()
 
-        for lower, upper in zip(*sides):
+        for lower, upper in zip(part(axis, 0, half), part(axis, 1, half)):
             for (rows_l, _), (rows_u, _) in zip(plane(axis, lower, 1), plane(axis, upper, 0)):
                 both = field[rows_l] + field[rows_u]
                 field[rows_l] = both
                 field[rows_u] = both
+        return copies
+
+    def finish(axis, half, copies):
         for side in range(2):
 
             @pl.when(exists[axis][side])
             def _():
                 copies[1 - side].wait_recv()
-                at = 0
-                for element in sides[side]:
+                at = half * outgoing.shape[2] // 2
+                for element in part(axis, side, half):
                     for rows, count in plane(axis, element, side):
                         field[rows] += arriving[axis, side, at:at + count]
                         at += count
                 copies[side].wait_send()
+
+    along_z = [begin(2, half) for half in range(2)]
+    along_y = []
+    for half in range(2):
+        finish(2, half, along_z[half])
+        along_y.append(begin(1, half))
+    for half in range(2):
+        finish(1, half, along_y[half])
+    finish(0, 0, begin(0, 0))
 
 
 def make_consistent(field, collective):
@@ -409,8 +424,8 @@
         scratch_shapes=[
             pltpu.VMEM((3, 2, face, channels), F32),
             pltpu.VMEM((3, 2, face, channels), F32),
-            pltpu.SemaphoreType.DMA((3, 2)),
-            pltpu.SemaphoreType.DMA((3, 2)),
+            pltpu.SemaphoreType.DMA((3, 2, 2)),
+            pltpu.SemaphoreType.DMA((3, 2, 2)),
         ],
         compiler_params=pltpu.CompilerParams(
             collective_id=collective, has_side_effects=True, vmem_limit_bytes=VMEM_BYTES

time: 125 us -> 123 us (0.984)
  Pallas kernels: 115 us -> 113 us
    pallas_call x2, Pallas kernels: 36.1 us -> 33.5 us  [make_consistent(): pl.pallas_call(functools.partial(exchange_kernel, devices), out_shape=jax...]
where the time goes in v4:
time: 123 us
  Pallas kernels  113 us (92%)
  local copies, waits for them, and re-layouts  9.27 us (8%)
    pallas_call x3, Pallas kernels, on_elements(): pl.pallas_call(kernel, grid_spec=pltpu.PrefetchScalarGridSpec(num_scalar_...  53.7 us
    pallas_call x2, Pallas kernels, make_consistent(): pl.pallas_call(functools.partial(exchange_kernel, devices), out_shape=jax...  33.5 us
    pallas_call x1, Pallas kernels, sum_over_devices(): pl.pallas_call(functools.partial(total_kernel, devices, scale), out_shape...  25.4 us
    unnamed x30, local copies, waits for them, and re-layouts  8.54 us

profile of v4, /device:TPU:0, one launch (start us, length us, event | category | flops | bytes accessed | tf_op | source)
XLA Modules:
  0.0 122.6 jit_solution(3715039354060229364)
XLA Ops:
  0.6 0.7 reshape.27.order
  1.4 0.0 copy-start
  1.4 1.6 %copy-done = f32[4096,128]{1,0:T(8,128)S(1)} copy-done((f32[4096,128]{1,0:T(8,128)S(1)}, f32[4096,128]{1,0:T(8,128)}, u32[]{:S(2)}) %copy-start) | copy-done | bytes 2097176
  3.0 0.9 copy-done.4
  3.9 0.9 copy-done.6
  4.8 0.7 copy-done.9
  5.5 0.7 copy-done.11
  6.1 11.5 %shard_map.161 = (f32[4096,128]{1,0:T(8,128)S(1)}, f32[4096,128]{1,0:T(8,128)S(1)}, f32[4096,128]{1,0:T(8,128)S(1)}) custom-call(s32[1,8]{1,0:T(1,128)S(1)} %copy-done.11, f32[4096,128]{1,0:T(8,128)S(1)} %copy-done, s32[8,1,512]{2,1,0:T(1,128)S(1)} %reshape.27.order, f32[256,128]{1,0:T(8,128)S(1)} %copy-done.4, f32[2,128,128]{2,1,0:T(8,128)S(1)} %copy-done.6, ...), custom_call_target="tpu_custom_call" | custom-call | flops 2952790016 | bytes 8388608 | tf_op jit(solution)/shard_map/pallas_call | solution.py:297
  17.7 0.0 copy-start.1
  17.7 0.0 copy-start.2
  17.7 0.0 copy-start.3
  17.7 0.0 copy-start.8
  17.7 17.5 %shard_map.162.gathered_ref = f32[4096,128]{1,0:T(8,128)S(1)} custom-call(f32[4096,128]{1,0:T(8,128)S(1)} %get-tuple-element.24.field_in), custom_call_target="tpu_custom_call" | custom-call | tf_op jit(solution)/shard_map/pallas_call | solution.py:419
  35.2 0.0 copy-done.1
  35.2 14.9 %shard_map.163 = (f32[4096,128]{1,0:T(8,128)}, f32[4096,128]{1,0:T(8,128)S(1)}, f32[4096,128]{1,0:T(8,128)S(1)}, f32[520,128]{1,0:T(8,128)S(1)}) custom-call(s32[1,8]{1,0:T(1,128)S(1)} %copy-done.11, f32[4096,128]{1,0:T(8,128)S(1)} %get-tuple-element.23.lattice_ref, f32[4096,128]{1,0:T(8,128)S(1)} %shard_map.162.gathered_ref, f32[4096,128]{1,0:T(8,128)S(1)} %copy-done.1, ...), custom_call_target="tpu_custom_call" | custom-call | flops 6442450944 | bytes 8388608 | tf_op jit(solution)/shard_map/pallas_call | solution.py:297
  50.1 16.0 %shard_map.164.around_ref = f32[4096,128]{1,0:T(8,128)S(1)} custom-call(f32[4096,128]{1,0:T(8,128)S(1)} %get-tuple-element.26.field_in), custom_call_target="tpu_custom_call" | custom-call | tf_op jit(solution)/shard_map/pallas_call | solution.py:419
  66.2 27.3 %shard_map.165 = (f32[4096,128]{1,0:T(8,128)}, f32[520,128]{1,0:T(8,128)S(1)}) custom-call(s32[1,8]{1,0:T(1,128)S(1)} %copy-done.11, f32[4096,128]{1,0:T(8,128)S(1)} %get-tuple-element.23.lattice_ref, f32[4096,128]{1,0:T(8,128)S(1)} %shard_map.164.around_ref, f32[4096,128]{1,0:T(8,128)S(1)} %get-tuple-element.27.summed_ref, ...), custom_call_target="tpu_custom_call" | custom-call | flops 8858370048 | bytes 8388608 | tf_op jit(solution)/shard_map/pallas_call | solution.py:297
  93.5 25.4 %shard_map.166 = (f32[256,128]{1,0:T(8,128)S(1)}, f32[256,128]{1,0:T(8,128)S(1)}, f32[3,128]{1,0:T(4,128)S(1)}, f32[256,128]{1,0:T(8,128)S(1)}, f32[256,128]{1,0:T(8,128)S(1)}, /*index=5*/f32[3,128]{1,0:T(4,128)S(1)}) custom-call(f32[520,128]{1,0:T(8,128)S(1)} %get-tuple-element.30.edge, f32[520,128]{1,0:T(8,128)S(1)} %get-tuple-element.31.node), custom_call_target="tpu_custom_call" | custom-call | tf_op jit(solution)/shard_map/pallas_call | solution.py:528
  118.8 0.7 copy.24
  119.5 0.7 copy.25
  120.2 0.6 copy.26
  120.7 0.7 copy.27
  121.4 0.7 copy.28
  122.0 0.6 copy.29
  (13 shorter events, 0.0 us)
Async XLA Ops:
  1.4 1.6 %copy-start = (f32[4096,128]{1,0:T(8,128)S(1)}, f32[4096,128]{1,0:T(8,128)}, u32[]{:S(2)}) copy-start(f32[4096,128]{1,0:T(8,128)} %feat.1) | copy-start | bytes 6291460
  3.0 0.9 copy-start.4
  3.9 0.9 copy-start.6
  4.8 0.7 copy-start.9
  5.5 0.7 copy-start.11
  17.7 17.5 %copy-start.1 = (f32[4096,128]{1,0:T(8,128)S(1)}, f32[4096,128]{1,0:T(8,128)}, u32[]{:S(2)}) copy-start(f32[4096,128]{1,0:T(8,128)} %cotangent.1) | copy-start | bytes 6291460
  17.7 17.5 %copy-start.2 = (f32[256,128]{1,0:T(8,128)S(1)}, f32[256,128]{1,0:T(8,128)}, u32[]{:S(2)}) copy-start(f32[256,128]{1,0:T(8,128)} %w_in.4) | copy-start | bytes 393220
  17.7 17.5 %copy-start.3 = (f32[2,128,128]{2,1,0:T(8,128)S(1)}, f32[2,128,128]{2,1,0:T(8,128)}, u32[]{:S(2)}) copy-start(f32[2,128,128]{2,1,0:T(8,128)} %w_mid.4) | copy-start | bytes 393220
  17.7 17.5 %copy-start.8 = (f32[3,128]{1,0:T(4,128)S(1)}, f32[3,128]{1,0:T(4,128)}, u32[]{:S(2)}) copy-start(f32[3,128]{1,0:T(4,128)} %bias.4) | copy-start | bytes 4612
  50.1 16.0 %copy-start.5 = (f32[256,128]{1,0:T(8,128)S(1)}, f32[256,128]{1,0:T(8,128)}, u32[]{:S(2)}) copy-start(f32[256,128]{1,0:T(8,128)} %w_in.5) | copy-start | bytes 393220
  50.1 16.0 %copy-start.7 = (f32[2,128,128]{2,1,0:T(8,128)S(1)}, f32[2,128,128]{2,1,0:T(8,128)}, u32[]{:S(2)}) copy-start(f32[2,128,128]{2,1,0:T(8,128)} %w_mid.5) | copy-start | bytes 393220
  50.1 16.0 %copy-start.10 = (f32[3,128]{1,0:T(4,128)S(1)}, f32[3,128]{1,0:T(4,128)}, u32[]{:S(2)}) copy-start(f32[3,128]{1,0:T(4,128)} %bias.5) | copy-start | bytes 4612
